TPU v7x, 32 devices: a whole 2x2x4 slice. The times are simulated.
32 devices in a mesh: parts: 2 (over y), row: 4 (over z), col: 2 (over x), freq: 2 (over core).
Axes of the slice: x: 2, y: 2, z: 4, core: 2. Of those that a mesh axis runs over, the one named last changes fastest.
Arguments:
- green: float32 [4, 2, 8192, 512], P('freq', None, ('parts', 'row', 'col')), parts along dimension 2, may hold values from -6 to 6
- weights: float32 [8], P(('parts', 'freq')), parts along dimension 0, may hold values from 0.5 to 2
- listed: int32 [64, 9], P(('parts', 'row', 'col')), parts along dimension 0, may hold values 0 or 1
Outputs:
- hessian: float32 [64, 9, 128, 128], P(('parts', 'row', 'col'), None, 'freq'), parts along dimension 0
There are 2 independent parts, one for each index of `parts`. A program takes and returns all parts, laid end to end along the dimension named above; each array names one. Nothing has to cross between parts.
All inputs are finite; a program needn't handle non-finite values. No bound on the sum of `listed` on one device may be relied on, other than what follows from the above.
Results may differ from a plain program's by a relative error of at most 0.00007.
Values sent between devices are 32-bit elements; how exact they have to be, the bound alone decides.
A program may use at most 192 MiB of HBM per device.

v0:
```python
import math

import jax
import jax.numpy as jnp
from jax import lax
from jax.sharding import PartitionSpec as P

B = 128
NS = 256
NR = 256
BPD = 4
K1 = 9
SPAN = 2


def from_behind(value, axis, steps):
    count = lax.axis_size(axis)
    leading, last = (max(0, -steps), min(count, count - steps))
    return lax.ppermute(value, axis, [(source, source + steps) for source in range(leading, last)])


def half_gram(row_panel, col_panel):
    re_row = row_panel[:, 0]
    im_row = row_panel[:, 1]
    re_col = col_panel[:, 0]
    im_col = col_panel[:, 1]
    left_side = jnp.concatenate(
        [jnp.concatenate([re_row, im_row], -1), jnp.concatenate([im_row, -re_row], -1)], 1
    )
    right_side = jnp.concatenate([re_col, im_col], -1)
    product = jnp.einsum("fxs,fys->fxy", left_side, right_side, precision=lax.Precision.HIGHEST)
    n = re_row.shape[1]
    return (product[:, :n], product[:, n:])


def gram_tiles(row_panel, col_panel, weights, listed_row):
    source_re, source_im = half_gram(row_panel[..., :NS], col_panel[..., :NS])
    recv_re, recv_im = half_gram(row_panel[..., NS:], col_panel[..., NS:])
    real_part = source_re * recv_re - source_im * recv_im
    weighted = jnp.einsum("f,fxy->xy", weights, real_part, precision=lax.Precision.HIGHEST)
    weighted = weighted * (1.0 / math.sqrt(NS * NR))
    n = weighted.shape[0]
    tile_set = weighted.reshape(n, K1, B).transpose(1, 0, 2)
    return tile_set * listed_row.astype(jnp.float32)[:, None, None]


def on_device(green, weights, listed):
    panels, freq_weights = (green, weights)
    row_count = B
    ahead = []
    for step in range(SPAN):
        ahead.append(from_behind(panels, ("row", "col"), -(step + 1)))
    columns = jnp.concatenate([panels] + ahead, axis=2)
    results = []
    for block in range(BPD):
        row_panel = lax.dynamic_slice_in_dim(panels, block * B, row_count, 2)
        col_panel = columns[:, :, block * B : block * B + K1 * B]
        results.append(gram_tiles(row_panel, col_panel, freq_weights, listed[block]))
    tile_stack = jnp.stack(results)
    return lax.psum_scatter(tile_stack, "freq", scatter_dimension=2, tiled=True)


def solution(mesh):
    in_specs = (
        P("freq", None, ("parts", "row", "col"), None),
        P(("parts", "freq")),
        P(("parts", "row", "col"), None),
    )
    out_specs = P(("parts", "row", "col"), None, "freq", None)
    return jax.shard_map(
        on_device, mesh=mesh, in_specs=in_specs, out_specs=out_specs, check_vma=False
    )
```

profile of v0, /device:TPU:0, one launch (start us, length us, event | category | flops | bytes accessed | tf_op | source)
XLA Modules:
  0.0 338.9 jit_solution(2349170843988133737)
XLA Ops:
  6.5 0.0 copy-start
  6.5 0.0 all-reduce.3.cloned.1.call-start
  6.5 4.9 %fusion.120 = (f32[2,2,512,512]{3,2,0,1:T(8,128)S(1)}, f32[2,2,1536,512]{3,2,0,1:T(8,128)}) fusion(f32[2,2,512,512]{3,2,1,0:T(8,128)} %param.3), kind=kLoop, calls=%fused_computation.177 | loop fusion | bytes 12582912 | tf_op args[0]
  11.4 1.3 collective-permute-start
  12.7 1.3 collective-permute-start.1
  14.0 0.0 copy-done.18
  14.0 0.5 convert_bitcast_fusion.3
  14.5 1.1 fusion.112
  15.7 1.6 slice_bitcast_fusion.31
  17.3 89.5 %collective-permute-done = f32[2,2,512,512]{3,2,0,1:T(8,128)S(1)} collective-permute-done((f32[2,2,512,512]{3,2,0,1:T(8,128)S(1)}, f32[2,2,512,512]{3,2,0,1:T(8,128)S(1)}, u32[]{:S(2)}, u32[]{:S(2)}) %collective-permute-start) | collective-permute-done | bytes 4194336 | tf_op jit(solution)/shard_map/ppermute | solution.py:19
  106.8 2.5 constant_dynamic-update-slice_fusion.1
  109.3 88.6 %collective-permute-done.1 = f32[2,2,512,512]{3,2,0,1:T(8,128)S(1)} collective-permute-done((f32[2,2,512,512]{3,2,0,1:T(8,128)S(1)}, f32[2,2,512,512]{3,2,0,1:T(8,128)S(1)}, u32[]{:S(2)}, u32[]{:S(2)}) %collective-permute-start.1) | collective-permute-done | bytes 4194336 | tf_op jit(solution)/shard_map/ppermute | solution.py:19
  197.9 2.5 constant_dynamic-update-slice_fusion
  200.4 26.5 %slice_bitcast_fusion.15 = (f32[2,1152,256]{2,1,0:T(8,128)}, f32[2,1152,256]{2,1,0:T(8,128)S(1)}, f32[2,1152,256]{2,1,0:T(8,128)}, f32[2,1152,256]{2,1,0:T(8,128...) fusion(f32[2,2,1536,512]{3,2,0,1:T(8,128)} %constant_dynamic-up, ...), kind=kLoop, calls=%fused_computation.47 | loop fusion | bytes 75497472 | tf_op jit(solution)/shard_map/squeeze | solution.py:25
  226.8 0.0 copy-start.6
  226.8 6.5 %fusion = f32[2,256,1152]{2,1,0:T(8,128)S(1)} fusion(f32[2,1152,256]{2,1,0:T(8,128)} %get-tuple-element.20, f32[2,1152,256]{2,1,0:T(8,128)} %get-tuple-element.5, f32[2,128,256]{2,1,0:T(8,128)S(1)} %get-tuple-element.37, f32[2,128,256]{2,1,0:T(8,128)S(1)} %get-tuple-element.36, f32[2,128,256]{2,1,0:T(8,128)S(1)} %get-tuple-element.21), kind=kOutput, calls=%fused_computation | convolution fusion | flops 3625844736 | bytes 7864320 | tf_op jit(solution)/shard_map/fxs,fys->fxy/dot_general | solution.py:31
  233.4 0.0 copy-done.6
  233.4 4.6 %fusion.4 = f32[2,256,1152]{2,1,0:T(8,128)S(1)} fusion(f32[2,1152,256]{2,1,0:T(8,128)S(1)} %get-tuple-element.18, f32[2,1152,256]{2,1,0:T(8,128)S(1)} %copy-done.6, f32[2,128,256]{2,1,0:T(8,128)S(1)} %get-tuple-element.43, f32[2,128,256]{2,1,0:T(8,128)S(1)} %get-tuple-element.34, f32[2,128,256]{2,1,0:T(8,128)S(1)} %get-tuple-element.35), kind=kOutput, calls=%fused_computation.4 | convolution fusion | flops 3625844736 | bytes 7864320 | tf_op jit(solution)/shard_map/fxs,fys->fxy/dot_general | solution.py:31
  238.0 0.2 fusion.35
  238.2 0.0 copy-done
  238.2 5.2 %fusion.42 = f32[1,128,1152]{2,0,1:T(1,128)S(1)} fusion(f32[2,128,1152]{2,1,0:T(8,128)S(1)} %fusion.35, f32[2]{0:T(128)S(1)} %copy-done), kind=kOutput, calls=%fused_computation.67 | convolution fusion | flops 3538944 | bytes 1769480 | tf_op jit(solution)/shard_map/f,fxy->xy/dot_general | solution.py:40
  243.4 0.8 copy.65
  244.3 0.0 copy-start.4
  244.4 0.0 copy-start.5
  244.4 0.0 copy-start.15
  244.4 0.0 copy-start.16
  244.4 0.0 copy-start.17
  244.4 7.4 %fusion.8 = f32[2,256,1152]{2,1,0:T(8,128)S(1)} fusion(f32[2,1152,256]{2,1,0:T(8,128)} %get-tuple-element.16, f32[2,1152,256]{2,1,0:T(8,128)} %get-tuple-element.17, f32[2,128,256]{2,1,0:T(8,128)} %get-tuple-element.42, f32[2,128,256]{2,1,0:T(8,128)} %get-tuple-element.32, f32[2,128,256]{2,1,0:T(8,128)} %get-tuple-element.33), kind=kOutput, calls=%fused_computation.8 | convolution fusion | flops 3625844736 | bytes 7864320 | tf_op jit(solution)/shard_map/fxs,fys->fxy/dot_general | solution.py:31
  251.8 0.0 copy-done.4
  251.8 0.0 copy-done.5
  251.8 0.0 copy-done.15
  251.8 0.0 copy-done.16
  251.8 0.0 copy-done.17
  251.8 4.6 %fusion.12 = f32[2,256,1152]{2,1,0:T(8,128)S(1)} fusion(f32[2,1152,256]{2,1,0:T(8,128)S(1)} %copy-done.4, f32[2,1152,256]{2,1,0:T(8,128)S(1)} %copy-done.5, f32[2,128,256]{2,1,0:T(8,128)S(1)} %copy-done.15, f32[2,128,256]{2,1,0:T(8,128)S(1)} %copy-done.16, f32[2,128,256]{2,1,0:T(8,128)S(1)} %copy-done.17), kind=kOutput, calls=%fused_computation.12 | convolution fusion | flops 3625844736 | bytes 7864320 | tf_op jit(solution)/shard_map/fxs,fys->fxy/dot_general | solution.py:31
  256.4 0.2 fusion.34
  256.6 5.9 %fusion.40 = f32[1,128,1152]{2,0,1:T(1,128)} fusion(f32[2,128,1152]{2,1,0:T(8,128)S(1)} %fusion.34, f32[2]{0:T(128)S(1)} %copy-done), kind=kOutput, calls=%fused_computation.65 | convolution fusion | flops 3538944 | bytes 1769480 | tf_op jit(solution)/shard_map/f,fxy->xy/dot_general | solution.py:40
  262.5 1.7 copy.67
  264.2 0.9 bitcast_multiply_fusion.2
  265.1 0.0 copy-start.14
  265.1 7.4 %fusion.16 = f32[2,256,1152]{2,1,0:T(8,128)S(1)} fusion(f32[2,1152,256]{2,1,0:T(8,128)} %get-tuple-element.12, f32[2,1152,256]{2,1,0:T(8,128)} %get-tuple-element.13, f32[2,128,256]{2,1,0:T(8,128)} %get-tuple-element.40, f32[2,128,256]{2,1,0:T(8,128)} %get-tuple-element.28, f32[2,128,256]{2,1,0:T(8,128)} %get-tuple-element.29), kind=kOutput, calls=%fused_computation.16 | convolution fusion | flops 3625844736 | bytes 7864320 | tf_op jit(solution)/shard_map/fxs,fys->fxy/dot_general | solution.py:31
  272.5 0.0 copy-done.2
  272.5 0.0 copy-done.3
  272.5 4.6 %fusion.20 = f32[2,256,1152]{2,1,0:T(8,128)S(1)} fusion(f32[2,1152,256]{2,1,0:T(8,128)S(1)} %copy-done.2, f32[2,1152,256]{2,1,0:T(8,128)S(1)} %copy-done.3, f32[2,128,256]{2,1,0:T(8,128)S(1)} %copy-done.12, f32[2,128,256]{2,1,0:T(8,128)S(1)} %copy-done.13, f32[2,128,256]{2,1,0:T(8,128)S(1)} %copy-done.14), kind=kOutput, calls=%fused_computation.20 | convolution fusion | flops 3625844736 | bytes 7864320 | tf_op jit(solution)/shard_map/fxs,fys->fxy/dot_general | solution.py:31
  277.1 0.2 fusion.33
  277.3 6.3 %fusion.38 = f32[1,128,1152]{2,0,1:T(1,128)} fusion(f32[2,128,1152]{2,1,0:T(8,128)S(1)} %fusion.33, f32[2]{0:T(128)S(1)} %copy-done), kind=kOutput, calls=%fused_computation.63 | convolution fusion | flops 3538944 | bytes 1769480 | tf_op jit(solution)/shard_map/f,fxy->xy/dot_general | solution.py:40
  283.7 1.5 copy.69
  285.1 0.9 bitcast_multiply_fusion.1
  286.0 7.4 %fusion.24 = f32[2,256,1152]{2,1,0:T(8,128)S(1)} fusion(f32[2,1152,256]{2,1,0:T(8,128)} %get-tuple-element.8, f32[2,1152,256]{2,1,0:T(8,128)} %get-tuple-element.9, f32[2,128,256]{2,1,0:T(8,128)} %get-tuple-element.38, f32[2,128,256]{2,1,0:T(8,128)} %get-tuple-element.24, f32[2,128,256]{2,1,0:T(8,128)} %get-tuple-element.25), kind=kOutput, calls=%fused_computation.24 | convolution fusion | flops 3625844736 | bytes 7864320 | tf_op jit(solution)/shard_map/fxs,fys->fxy/dot_general | solution.py:31
  293.4 4.6 %fusion.28 = f32[2,256,1152]{2,1,0:T(8,128)S(1)} fusion(f32[2,1152,256]{2,1,0:T(8,128)S(1)} %get-tuple-element.6, f32[2,1152,256]{2,1,0:T(8,128)S(1)} %copy-done.1, f32[2,128,256]{2,1,0:T(8,128)S(1)} %copy-done.9, f32[2,128,256]{2,1,0:T(8,128)S(1)} %copy-done.10, f32[2,128,256]{2,1,0:T(8,128)S(1)} %copy-done.11), kind=kOutput, calls=%fused_computation.28 | convolution fusion | flops 3625844736 | bytes 7864320 | tf_op jit(solution)/shard_map/fxs,fys->fxy/dot_general | solution.py:31
  298.0 0.2 fusion.32
  298.2 0.0 copy-start.7
  298.2 5.4 %fusion.36 = f32[1,128,1152]{2,0,1:T(1,128)S(1)} fusion(f32[2,128,1152]{2,1,0:T(8,128)S(1)} %fusion.32, f32[2]{0:T(128)S(1)} %copy-done), kind=kOutput, calls=%fused_computation.61 | convolution fusion | flops 3538944 | bytes 1769480 | tf_op jit(solution)/shard_map/f,fxy->xy/dot_general | solution.py:40
  303.6 0.0 copy-start.8
  303.7 0.7 copy.71
  304.4 0.7 multiply_bitcast_fusion.2
  305.1 0.1 multiply_bitcast_fusion
  305.3 0.2 pad_maximum_fusion
  305.5 2.7 copy.62
  308.2 0.0 all-reduce.3.cloned.1.call-update
  308.2 0.6 copy-done.19
  308.9 0.6 dynamic-slice
  310.1 19.2 %all-reduce.3.cloned.1.call-done = f32[4,9,128,128]{3,0,1,2:T(4,128)} async-done(((f32[4,9,128,128]{3,0,1,2:T(4,128)}), f32[4,9,128,128]{3,0,1,2:T(4,128)}) %all-reduce.3.cloned.1.call-update) | async-done | bytes 2359312
  329.3 1.4 constant_dynamic-slice_fusion
  330.7 1.2 copy.63
  (21 shorter events, 0.1 us)
Async XLA Ops:
  6.5 231.6 %copy-start = (f32[2]{0:T(128)S(1)}, f32[2]{0:T(128)}, u32[]{:S(2)}) copy-start(f32[2]{0:T(128)} %param.4) | copy-start | bytes 28
  6.5 7.5 %copy-start.18 = (s32[4,9]{1,0:T(4,128)S(1)}, s32[4,9]{1,0:T(4,128)}, u32[]{:S(2)}) copy-start(s32[4,9]{1,0:T(4,128)} %param.5) | copy-start | bytes 436
  6.5 322.8 %all-reduce.3.cloned.1.call-start = ((), (), s32[]{:S(2)}) async-start(), calls=%async_computation | async-start | bytes 4718592
  11.4 95.4 %collective-permute-start = (f32[2,2,512,512]{3,2,0,1:T(8,128)S(1)}, f32[2,2,512,512]{3,2,0,1:T(8,128)S(1)}, u32[]{:S(2)}, u32[]{:S(2)}) collective-permute-start(f32[2,2,512,512]{3,2,0,1:T(8,128)S(1)} %get-tuple-element.45), channel_id=1, source_target_pairs={{2,0},{4,2},{6,4},{8,6},{10,8},{12,10},{14,12},{3,1},{5,3},{7,5},{... | collective-permute-start | bytes 12582920 | tf_op jit(solution)/shard_map/ppermute | solution.py:19
  12.7 185.2 %collective-permute-start.1 = (f32[2,2,512,512]{3,2,0,1:T(8,128)S(1)}, f32[2,2,512,512]{3,2,0,1:T(8,128)S(1)}, u32[]{:S(2)}, u32[]{:S(2)}) collective-permute-start(f32[2,2,512,512]{3,2,0,1:T(8,128)S(1)} %get-tuple-element.45), channel_id=1, source_target_pairs={{4,0},{6,2},{8,4},{10,6},{12,8},{14,10},{5,1},{7,3},{9,5},{11,7},{... | collective-permute-start | bytes 12582920 | tf_op jit(solution)/shard_map/ppermute | solution.py:19
  226.8 6.5 %copy-start.6 = (f32[2,1152,256]{2,1,0:T(8,128)S(1)}, f32[2,1152,256]{2,1,0:T(8,128)}, u32[]{:S(2)}) copy-start(f32[2,1152,256]{2,1,0:T(8,128)} %get-tuple-element.19) | copy-start | bytes 7077892
  244.3 7.4 %copy-start.4 = (f32[2,1152,256]{2,1,0:T(8,128)S(1)}, f32[2,1152,256]{2,1,0:T(8,128)}, u32[]{:S(2)}) copy-start(f32[2,1152,256]{2,1,0:T(8,128)} %get-tuple-element.14) | copy-start | bytes 7077892
  244.4 7.4 %copy-start.5 = (f32[2,1152,256]{2,1,0:T(8,128)S(1)}, f32[2,1152,256]{2,1,0:T(8,128)}, u32[]{:S(2)}) copy-start(f32[2,1152,256]{2,1,0:T(8,128)} %get-tuple-element.15) | copy-start | bytes 7077892
  244.4 7.4 %copy-start.15 = (f32[2,128,256]{2,1,0:T(8,128)S(1)}, f32[2,128,256]{2,1,0:T(8,128)}, u32[]{:S(2)}) copy-start(f32[2,128,256]{2,1,0:T(8,128)} %get-tuple-element.41) | copy-start | bytes 786436
  244.4 7.4 %copy-start.16 = (f32[2,128,256]{2,1,0:T(8,128)S(1)}, f32[2,128,256]{2,1,0:T(8,128)}, u32[]{:S(2)}) copy-start(f32[2,128,256]{2,1,0:T(8,128)} %get-tuple-element.30) | copy-start | bytes 786436
  244.4 7.4 %copy-start.17 = (f32[2,128,256]{2,1,0:T(8,128)S(1)}, f32[2,128,256]{2,1,0:T(8,128)}, u32[]{:S(2)}) copy-start(f32[2,128,256]{2,1,0:T(8,128)} %get-tuple-element.31) | copy-start | bytes 786436
  265.1 7.4 %copy-start.2 = (f32[2,1152,256]{2,1,0:T(8,128)S(1)}, f32[2,1152,256]{2,1,0:T(8,128)}, u32[]{:S(2)}) copy-start(f32[2,1152,256]{2,1,0:T(8,128)} %get-tuple-element.10) | copy-start | bytes 7077892
  265.1 7.4 %copy-start.3 = (f32[2,1152,256]{2,1,0:T(8,128)S(1)}, f32[2,1152,256]{2,1,0:T(8,128)}, u32[]{:S(2)}) copy-start(f32[2,1152,256]{2,1,0:T(8,128)} %get-tuple-element.11) | copy-start | bytes 7077892
  265.1 7.4 %copy-start.12 = (f32[2,128,256]{2,1,0:T(8,128)S(1)}, f32[2,128,256]{2,1,0:T(8,128)}, u32[]{:S(2)}) copy-start(f32[2,128,256]{2,1,0:T(8,128)} %get-tuple-element.39) | copy-start | bytes 786436
  265.1 7.4 %copy-start.13 = (f32[2,128,256]{2,1,0:T(8,128)S(1)}, f32[2,128,256]{2,1,0:T(8,128)}, u32[]{:S(2)}) copy-start(f32[2,128,256]{2,1,0:T(8,128)} %get-tuple-element.26) | copy-start | bytes 786436
  265.1 7.4 %copy-start.14 = (f32[2,128,256]{2,1,0:T(8,128)S(1)}, f32[2,128,256]{2,1,0:T(8,128)}, u32[]{:S(2)}) copy-start(f32[2,128,256]{2,1,0:T(8,128)} %get-tuple-element.27) | copy-start | bytes 786436
  286.0 7.4 %copy-start.1 = (f32[2,1152,256]{2,1,0:T(8,128)S(1)}, f32[2,1152,256]{2,1,0:T(8,128)}, u32[]{:S(2)}) copy-start(f32[2,1152,256]{2,1,0:T(8,128)} %get-tuple-element.7) | copy-start | bytes 7077892
  286.0 7.4 %copy-start.9 = (f32[2,128,256]{2,1,0:T(8,128)S(1)}, f32[2,128,256]{2,1,0:T(8,128)}, u32[]{:S(2)}) copy-start(f32[2,128,256]{2,1,0:T(8,128)} %get-tuple-element.44) | copy-start | bytes 786436
  286.0 7.4 %copy-start.10 = (f32[2,128,256]{2,1,0:T(8,128)S(1)}, f32[2,128,256]{2,1,0:T(8,128)}, u32[]{:S(2)}) copy-start(f32[2,128,256]{2,1,0:T(8,128)} %get-tuple-element.22) | copy-start | bytes 786436
  286.0 7.4 %copy-start.11 = (f32[2,128,256]{2,1,0:T(8,128)S(1)}, f32[2,128,256]{2,1,0:T(8,128)}, u32[]{:S(2)}) copy-start(f32[2,128,256]{2,1,0:T(8,128)} %get-tuple-element.23) | copy-start | bytes 786436
  298.2 6.2 %copy-start.7 = (f32[128,1152]{0,1:T(8,128)S(1)}, f32[128,1152]{0,1:T(8,128)}, u32[]{:S(2)}) copy-start(f32[128,1152]{0,1:T(8,128)} %bitcast_multiply_fusion.2) | copy-start | bytes 1769476
  303.6 1.5 copy-start.8
  308.2 0.7 copy-start.19
Sparse Core Ops, SparseCore 0:
  308.4 20.9 all-reduce.2
where the time goes:
time: 342 us; the launch traced here: 339 us
  waiting for transfers between devices  197 us (58%)
  matrix products  69.8 us (20%)
  local copies, waits for them, and re-layouts  49.1 us (14%)
  between operations  14.7 us (4%)
  other arithmetic  5.37 us (2%)
    ppermute x2, waiting for transfers between devices, from_behind(): lax.ppermute(value, axis, [(source, source + steps) for source in range(l...  178 us
    dot_general x8, matrix products, half_gram(): jnp.einsum('fxs,fys->fxy', left_side, right_side, precision=lax.Precision...  46.8 us
    squeeze x1, local copies, waits for them, and re-layouts, half_gram(): re_col = col_panel[:, 0]  26.5 us
    dot_general x4, matrix products, gram_tiles(): jnp.einsum('f,fxy->xy', weights, real_part, precision=lax.Precision.HIGHEST)  23 us
    unnamed x2, waiting for transfers between devices  19.2 us
    unnamed x44, local copies, waits for them, and re-layouts  10 us
  transfers between devices with their start and end apart: 3, of which 3 were waited for; matrix products, arithmetic and copies ran while one was open for 2% of the time, Pallas kernels for 0%

commit v1 on v0

v1 whole, which is shorter than its diff:
```python
import functools
import math

import jax
import jax.numpy as jnp
from jax import lax
from jax.experimental import pallas as pl
from jax.experimental.pallas import tpu as pltpu
from jax.sharding import PartitionSpec as P

B = 128
Q = 4
K1 = 9
MESH = pl.DeviceIdType.MESH

OWN, OTH, PAR, NB1, NB2 = 0, 4, 8, 12, 16
T_O, T_W, T_A, T_C, T_B, T_END = 0, 10, 26, 36, 52, 62


def stair(r, c):
    return r * (r + 1) // 2 + c


def kernel(rows_n, cols_n, green, weights, listed, out, raw, hi, lo, part, cx, summed, got_m, got_n,
           loc_sem, r_send, r_recv, a_send, a_recv, b_send, b_recv, c_send, c_recv, m_send, m_recv):
    count = rows_n * cols_n
    groups = count // 2
    nsr = green.shape[3]
    ns = nsr // 2
    core = lax.axis_index("freq")
    d = lax.axis_index("row") * cols_n + lax.axis_index("col")
    p = lax.rem(d, 2)
    g = d // 2
    first = p == 0
    up = g < groups - 1
    dn = g > 0
    send1 = jnp.logical_or(jnp.logical_and(first, dn), jnp.logical_and(p == 1, up))
    send2 = jnp.logical_or(jnp.logical_and(first, up), jnp.logical_and(p == 1, dn))

    def at(e):
        e = jnp.clip(e, 0, count - 1)
        return {"row": e // cols_n, "col": lax.rem(e, cols_n)}

    mate = at(d + 1 - 2 * p)
    twin = {"freq": 1 - core}
    to1 = at(d - 2 + 4 * p)
    to2 = at(d + 2 - 4 * p)
    diag = at(d - 1 + 2 * p)

    def remote(src, dst, s, r, dev):
        return pltpu.make_async_remote_copy(
            src_ref=src, dst_ref=dst, send_sem=s, recv_sem=r, device_id=dev, device_id_type=MESH)

    def local(f, j):
        return pltpu.make_async_copy(
            green.at[jnp.where(f == 0, p, 1 - p), :, pl.ds(j * B, B), :], raw.at[f * Q + j], loc_sem.at[f * Q + j])

    def copy_r(j):
        return remote(green.at[1 - p, :, pl.ds(j * B, B), :], raw.at[PAR + j], r_send.at[j], r_recv.at[j], mate)

    def copy_a(j):
        return remote(green.at[p, :, pl.ds(j * B, B), :], raw.at[NB1 + j], a_send.at[j], a_recv.at[j], to1)

    def copy_b(j):
        return remote(raw.at[PAR + j], raw.at[NB2 + j], b_send.at[j], b_recv.at[j], to2)

    for f in range(2):
        for j in range(Q):
            local(f, j).start()

    barrier = pltpu.get_barrier_semaphore()
    pl.semaphore_signal(barrier, inc=1, device_id=twin, device_id_type=MESH)
    pl.semaphore_signal(barrier, inc=1, device_id=mate, device_id_type=MESH)

    @pl.when(send1)
    def _():
        pl.semaphore_signal(barrier, inc=1, device_id=to1, device_id_type=MESH)

    @pl.when(send2)
    def _():
        pl.semaphore_signal(barrier, inc=1, device_id=to2, device_id_type=MESH)

    @pl.when(send1)
    def _():
        pl.semaphore_signal(barrier, inc=1, device_id=diag, device_id_type=MESH)

    pl.semaphore_wait(barrier, 2 + 2 * send1.astype(jnp.int32) + send2.astype(jnp.int32))

    for j in reversed(range(Q)):
        copy_r(j).start()

        @pl.when(send1)
        def _():
            copy_a(j).start()

    def split(slot):
        for part_i in range(2):
            for h in range(2):
                x = raw[slot, part_i, :, h * ns:(h + 1) * ns]
                xh = x.astype(jnp.bfloat16)
                xl = (x - xh.astype(jnp.float32)).astype(jnp.bfloat16)
                base = h * 2 * ns
                a = base + part_i * ns
                b = base + (1 - part_i) * ns
                hi[slot, 0:B, a:a + ns] = xh
                lo[slot, 0:B, a:a + ns] = xl
                hi[slot, B:2 * B, b:b + ns] = -xh if part_i == 1 else xh
                lo[slot, B:2 * B, b:b + ns] = -xl if part_i == 1 else xl

    def gram(rs, cs, h):
        k = slice(h * 2 * ns, (h + 1) * 2 * ns)
        xh, xl, yh, yl = hi[rs, 0:B, k], lo[rs, 0:B, k], hi[cs, :, k], lo[cs, :, k]

        def dot(x, y):
            return lax.dot_general(x, y, (((1,), (1,)), ((), ())), preferred_element_type=jnp.float32)

        return dot(xh, yh) + (dot(xh, yl) + dot(xl, yh))

    def tile(rs, cs):
        s = gram(rs, cs, 0)
        r = gram(rs, cs, 1)
        return s[:, :B] * r[:, :B] - s[:, B:] * r[:, B:]

    scale = 1.0 / math.sqrt(ns * (nsr - ns))
    w_own = weights[p] * scale
    w_oth = weights[1 - p] * scale

    def put(slot, value):
        part[0, slot] = value[:B // 2]
        part[1, slot] = value[B // 2:]

    def cross(start, stop, row_of, col_of, slot_of):
        def body(t, _):
            put(slot_of(t), tile(row_of(t), col_of(t)) * w_own)
            return 0
        lax.fori_loop(start, stop, body, 0)

    def cx_copy(i, a, b):
        return remote(part.at[1 - core, a:b], cx.at[a:b], c_send.at[i], c_recv.at[i], twin)

    def cx_sum(i, a, b):
        cx_copy(i, a, b).wait()

        def body(t, _):
            summed[t] = part[core, t] + cx[t]
            return 0
        lax.fori_loop(a, b, body, 0)

    for f in range(2):
        for j in range(Q):
            local(f, j).wait()

    def split_own(s, _):
        split(s)
        return 0
    lax.fori_loop(0, 2 * Q, split_own, 0)

    for j in range(Q):
        def body(i, _, j=j):
            put(T_O + stair(j, i), tile(OWN + i, OWN + j) * w_own + tile(OTH + i, OTH + j) * w_oth)
            return 0
        lax.fori_loop(0, j + 1, body, 0)
    cx_copy(0, T_O, T_W).start()

    def zero(slot):
        raw[slot] = jnp.zeros(raw.shape[1:], jnp.float32)

    for j in reversed(range(Q)):
        copy_r(j).wait_recv()

        @pl.when(send2)
        def _():
            copy_b(j).start()

        split(PAR + j)
        cross(0, Q,
              lambda t: jnp.where(first, OWN + t, PAR + j),
              lambda t: jnp.where(first, PAR + j, OWN + t),
              lambda t: T_W + jnp.where(first, t * Q + j, j * Q + t))

        @pl.when(send2)
        def _():
            copy_a(j).wait_recv()

        @pl.when(jnp.logical_not(send2))
        def _():
            zero(NB1 + j)

        split(NB1 + j)
        cross(j, Q,
              lambda t: jnp.where(first, OWN, NB1) + t,
              lambda t: jnp.where(first, NB1, OWN) + j,
              lambda t: T_A + stair(t, j))

    cx_copy(1, T_W, T_A).start()
    cx_copy(2, T_A, T_C).start()

    def c_even(t, _):
        put(T_C + t, tile(PAR + t // Q, NB1 + lax.rem(t, Q)) * w_own)
        return 0
    lax.fori_loop(0, jnp.where(first, Q * Q, 0), c_even, 0)

    cx_sum(1, T_W, T_A)
    cx_sum(2, T_A, T_C)

    @pl.when(p == 1)
    def _():
        remote(summed.at[T_W:T_A], got_m, m_send.at[0], m_recv.at[0], mate).start()

    @pl.when(jnp.logical_and(p == 1, dn))
    def _():
        remote(summed.at[T_A:T_C], got_n.at[1], m_send.at[2], m_recv.at[2], to2).start()

    for j in reversed(range(Q)):
        @pl.when(send1)
        def _():
            copy_b(j).wait_recv()

        @pl.when(jnp.logical_not(send1))
        def _():
            zero(NB2 + j)

        split(NB2 + j)
        cross(0, jnp.where(first, 0, Q),
              lambda t: OWN + t,
              lambda t: NB2 + j,
              lambda t: T_C + t * Q + j)
        cross(j, Q,
              lambda t: jnp.where(first, NB2, PAR) + t,
              lambda t: jnp.where(first, PAR, NB2) + j,
              lambda t: T_B + stair(t, j))

    cx_copy(3, T_C, T_B).start()
    cx_copy(4, T_B, T_END).start()

    def flag(r, k):
        return listed[r, k].astype(jnp.float32)

    cx_copy(0, T_O, T_W).wait()
    for j in range(Q):
        for i in range(j + 1):
            s = T_O + stair(j, i)
            out[i, j - i] = (part[core, s] + cx[s]) * flag(i, j - i)

    cx_sum(3, T_C, T_B)

    @pl.when(first)
    def _():
        remote(summed.at[T_C:T_B], got_m, m_send.at[0], m_recv.at[0], mate).start()

    cx_sum(4, T_B, T_END)

    @pl.when(p == 1)
    def _():
        remote(summed.at[T_B:T_END], got_n.at[0], m_send.at[1], m_recv.at[1], mate).start()

    @pl.when(jnp.logical_and(first, dn))
    def _():
        remote(summed.at[T_B:T_END], got_n.at[0], m_send.at[1], m_recv.at[1], diag).start()

    remote(summed.at[T_W:T_A], got_m, m_send.at[0], m_recv.at[0], mate).wait_recv()
    mine = jnp.where(first, T_W, T_C)
    for r in range(Q):
        for c in range(Q):
            out[r, Q + c - r] = (summed[mine + r * Q + c] + got_m[r * Q + c]) * flag(r, Q + c - r)

    n_copy = remote(summed.at[T_B:T_END], got_n.at[0], m_send.at[1], m_recv.at[1], mate)
    n_copy2 = remote(summed.at[T_A:T_C], got_n.at[1], m_send.at[2], m_recv.at[2], to2)

    @pl.when(first)
    def _():
        n_copy.wait_recv()
        for r in range(Q):
            for c in range(r + 1):
                s = stair(r, c)
                out[r, 2 * Q + c - r] = (summed[T_A + s] + got_n[0, s]) * flag(r, 2 * Q + c - r)

    @pl.when(jnp.logical_and(p == 1, up))
    def _():
        n_copy.wait_recv()
        n_copy2.wait_recv()
        for r in range(Q):
            for c in range(r + 1):
                s = stair(r, c)
                out[r, 2 * Q + c - r] = (got_n[0, s] + got_n[1, s]) * flag(r, 2 * Q + c - r)

    @pl.when(jnp.logical_and(p == 1, jnp.logical_not(up)))
    def _():
        for r in range(Q):
            for c in range(r + 1):
                out[r, 2 * Q + c - r] = jnp.zeros((B // 2, B), jnp.float32)

    for j in range(Q):
        copy_r(j).wait_send()

        @pl.when(send1)
        def _():
            copy_a(j).wait_send()

        @pl.when(send2)
        def _():
            copy_b(j).wait_send()

    remote(summed.at[T_W:T_A], got_m, m_send.at[0], m_recv.at[0], mate).wait_send()

    @pl.when(jnp.logical_or(p == 1, dn))
    def _():
        n_copy.wait_send()

    @pl.when(jnp.logical_and(p == 1, dn))
    def _():
        n_copy2.wait_send()


def solution(mesh):
    in_specs = (
        P("freq", None, ("parts", "row", "col"), None),
        P(("parts", "freq")),
        P(("parts", "row", "col"), None),
    )
    out_specs = P(("parts", "row", "col"), None, "freq", None)
    rows_n, cols_n = mesh.shape["row"], mesh.shape["col"]

    def on_device(green, weights, listed):
        nsr = green.shape[3]
        dma = pltpu.SemaphoreType.DMA
        return pl.pallas_call(
            functools.partial(kernel, rows_n, cols_n),
            out_shape=jax.ShapeDtypeStruct((Q, K1, B // 2, B), jnp.float32),
            in_specs=[
                pl.BlockSpec(memory_space=pl.ANY),
                pl.BlockSpec(memory_space=pltpu.SMEM),
                pl.BlockSpec(memory_space=pltpu.SMEM),
            ],
            out_specs=pl.BlockSpec(memory_space=pltpu.VMEM),
            scratch_shapes=[
                pltpu.VMEM((5 * Q, 2, B, nsr), jnp.float32),
                pltpu.VMEM((5 * Q, 2 * B, 2 * nsr), jnp.bfloat16),
                pltpu.VMEM((5 * Q, 2 * B, 2 * nsr), jnp.bfloat16),
                pltpu.VMEM((2, T_END, B // 2, B), jnp.float32),
                pltpu.VMEM((T_END, B // 2, B), jnp.float32),
                pltpu.VMEM((T_END, B // 2, B), jnp.float32),
                pltpu.VMEM((T_A - T_W, B // 2, B), jnp.float32),
                pltpu.VMEM((2, T_C - T_A, B // 2, B), jnp.float32),
                dma((2 * Q,)),
                dma((Q,)), dma((Q,)), dma((Q,)), dma((Q,)), dma((Q,)), dma((Q,)),
                dma((5,)), dma((5,)), dma((3,)), dma((3,)),
            ],
            compiler_params=pltpu.CompilerParams(
                collective_id=0, has_side_effects=True, vmem_limit_bytes=56 * 1024 * 1024),
        )(green, weights, listed)

    return jax.shard_map(on_device, mesh=mesh, in_specs=in_specs, out_specs=out_specs, check_vma=False)
```

time: 342 us -> 98.2 us (0.29)
  waiting for transfers between devices: 197 us -> 0 us
  Pallas kernels: 0 us -> 95.6 us
  matrix products: 69.8 us -> 0 us
  local copies, waits for them, and re-layouts: 49.1 us -> 2.41 us
  between operations: 14.7 us -> 0.01 us
  other arithmetic: 5.37 us -> 0 us
    ppermute x2 -> x0, waiting for transfers between devices: 178 us -> none  [from_behind(): lax.ppermute(value, axis, [(source, source + steps) for source in range(l...]
    pallas_call x0 -> x1, Pallas kernels: none -> 95.6 us  [on_device(): pl.pallas_call(functools.partial(kernel, rows_n, cols_n), out_shape=jax.S...]
    dot_general x12 -> x0, matrix products: 69.8 us -> none  [the longest x8 46.8 us: half_gram(): jnp.einsum('fxs,fys->fxy', left_side, right_side, precision=lax.Precision...]
    squeeze x2 -> x0, local copies, waits for them, and re-layouts: 28.1 us -> none  [the longest x1 26.5 us: half_gram(): re_col = col_panel[:, 0]]
    unnamed x2 -> x0, waiting for transfers between devices: 19.2 us -> none
    unnamed x44 -> x1, local copies, waits for them, and re-layouts: 10 us -> 2.41 us
    dot_general x4 -> x0, local copies, waits for them, and re-layouts: 4.67 us -> none  [gram_tiles(): jnp.einsum('f,fxy->xy', weights, real_part, precision=lax.Precision.HIGHEST)]
  transfers between devices with their start and end apart: 3 -> 0, of which waited for: 3 -> 0; matrix products, arithmetic and copies ran while one was open for 2% -> 0% of each run, Pallas kernels for 0% -> 0%
where the time goes in v1:
time: 98.2 us; the launch traced here: 98 us
  Pallas kernels  95.6 us (97%)
  local copies, waits for them, and re-layouts  2.41 us (2%)
    pallas_call x1, Pallas kernels, on_device(): pl.pallas_call(functools.partial(kernel, rows_n, cols_n), out_shape=jax.S...  95.6 us
    unnamed x1, local copies, waits for them, and re-layouts  2.41 us

profile of v1, /device:TPU:0, one launch (start us, length us, event | category | flops | bytes accessed | tf_op | source)
XLA Modules:
  0.0 98.0 jit_solution(14980832199564674918)
XLA Ops:
  0.0 95.6 %shard_map.37 = f32[4,9,64,128]{3,2,1,0:T(8,128)} custom-call(f32[2,2,512,512]{3,2,1,0:T(8,128)} %green.1, f32[2]{0:T(128)} %weights.1, s32[4,9]{1,0:T(4,128)} %listed.1), custom_call_target="tpu_custom_call" | custom-call | tf_op jit(solution)/shard_map/pallas_call | solution.py:327
  95.6 2.4 %copy.5 = f32[4,9,64,128]{3,2,1,0:T(8,128)} copy(f32[4,9,64,128]{3,2,1,0:T(8,128)} %shard_map.37) | data formatting | bytes 2359296

commit v2 on v1

--- a/solution.py
+++ b/solution.py
@@ -19,6 +19,10 @@
 
 def stair(r, c):
     return r * (r + 1) // 2 + c
+
+
+def late(r, c):
+    return (Q - 1 - c) * (Q - c) // 2 + r - c
 
 
 def kernel(rows_n, cols_n, green, weights, listed, out, raw, hi, lo, part, cx, summed, got_m, got_n,
@@ -55,14 +59,19 @@
         return pltpu.make_async_copy(
             green.at[jnp.where(f == 0, p, 1 - p), :, pl.ds(j * B, B), :], raw.at[f * Q + j], loc_sem.at[f * Q + j])
 
-    def copy_r(j):
-        return remote(green.at[1 - p, :, pl.ds(j * B, B), :], raw.at[PAR + j], r_send.at[j], r_recv.at[j], mate)
+    H = B // 2
+
+    def copy_r(j, h):
+        return remote(green.at[1 - p, :, pl.ds(j * B + h * H, H), :], raw.at[PAR + j, :, pl.ds(h * H, H), :],
+                      r_send.at[2 * j + h], r_recv.at[2 * j + h], mate)
 
     def copy_a(j):
         return remote(green.at[p, :, pl.ds(j * B, B), :], raw.at[NB1 + j], a_send.at[j], a_recv.at[j], to1)
 
-    def copy_b(j):
-        return remote(raw.at[PAR + j], raw.at[NB2 + j], b_send.at[j], b_recv.at[j], to2)
+    def copy_b(j, h):
+        half = pl.ds(h * H, H)
+        return remote(raw.at[PAR + j, :, half, :], raw.at[NB2 + j, :, half, :],
+                      b_send.at[2 * j + h], b_recv.at[2 * j + h], to2)
 
     for f in range(2):
         for j in range(Q):
@@ -87,7 +96,8 @@
     pl.semaphore_wait(barrier, 2 + 2 * send1.astype(jnp.int32) + send2.astype(jnp.int32))
 
     for j in reversed(range(Q)):
-        copy_r(j).start()
+        copy_r(j, 0).start()
+        copy_r(j, 1).start()
 
         @pl.when(send1)
         def _():
@@ -135,16 +145,16 @@
             return 0
         lax.fori_loop(start, stop, body, 0)
 
-    def cx_copy(i, a, b):
-        return remote(part.at[1 - core, a:b], cx.at[a:b], c_send.at[i], c_recv.at[i], twin)
-
-    def cx_sum(i, a, b):
-        cx_copy(i, a, b).wait()
+    def cx_copy(i, a, n):
+        return remote(part.at[1 - core, pl.ds(a, n)], cx.at[pl.ds(a, n)], c_send.at[i], c_recv.at[i], twin)
+
+    def cx_sum(i, a, n):
+        cx_copy(i, a, n).wait()
 
         def body(t, _):
-            summed[t] = part[core, t] + cx[t]
+            summed[a + t] = part[core, a + t] + cx[a + t]
             return 0
-        lax.fori_loop(a, b, body, 0)
+        lax.fori_loop(0, n, body, 0)
 
     for f in range(2):
         for j in range(Q):
@@ -160,26 +170,49 @@
             put(T_O + stair(j, i), tile(OWN + i, OWN + j) * w_own + tile(OTH + i, OTH + j) * w_oth)
             return 0
         lax.fori_loop(0, j + 1, body, 0)
-    cx_copy(0, T_O, T_W).start()
+    cx_copy(0, T_O, T_W - T_O).start()
 
     def zero(slot):
         raw[slot] = jnp.zeros(raw.shape[1:], jnp.float32)
 
+    n_full, n_tri = Q * Q, T_C - T_A
+    away = jnp.where(first, T_C, T_W)
+    kept = jnp.where(first, T_W, T_C)
+
+    def send_m():
+        return remote(summed.at[pl.ds(away, n_full)], got_m, m_send.at[0], m_recv.at[0], mate)
+
+    def send_n(i, dev):
+        a, n = ((0, n_tri - Q), (n_tri - Q, Q))[i]
+        return remote(summed.at[pl.ds(T_B + a, n)], got_n.at[0, pl.ds(a, n)], m_send.at[1 + i], m_recv.at[1 + i], dev)
+
+    def send_a():
+        return remote(summed.at[pl.ds(T_A, n_tri)], got_n.at[1], m_send.at[3], m_recv.at[3], to2)
+
+    def start_n(i):
+        @pl.when(p == 1)
+        def _():
+            send_n(i, mate).start()
+
+        @pl.when(jnp.logical_and(first, dn))
+        def _():
+            send_n(i, diag).start()
+
+    def flag(r, k):
+        return listed[r, k].astype(jnp.float32)
+
     for j in reversed(range(Q)):
-        copy_r(j).wait_recv()
+        for h in range(2):
+            copy_r(j, h).wait_recv()
+
+            @pl.when(send2)
+            def _():
+                copy_b(j, h).start()
+
+        split(PAR + j)
 
         @pl.when(send2)
         def _():
-            copy_b(j).start()
-
-        split(PAR + j)
-        cross(0, Q,
-              lambda t: jnp.where(first, OWN + t, PAR + j),
-              lambda t: jnp.where(first, PAR + j, OWN + t),
-              lambda t: T_W + jnp.where(first, t * Q + j, j * Q + t))
-
-        @pl.when(send2)
-        def _():
             copy_a(j).wait_recv()
 
         @pl.when(jnp.logical_not(send2))
@@ -187,101 +220,99 @@
             zero(NB1 + j)
 
         split(NB1 + j)
+
+        def cr(t):
+            return jnp.where(t < Q - j, j, t - (Q - j) + j + 1)
+
+        def cc(t):
+            return jnp.where(t < Q - j, j + t, j)
+
+        cross(0, jnp.where(first, 2 * (Q - j) - 1, Q),
+              lambda t: jnp.where(first, PAR + cr(t), PAR + j),
+              lambda t: jnp.where(first, NB1 + cc(t), OWN + t),
+              lambda t: jnp.where(first, T_C + cr(t) * Q + cc(t), T_W + j * Q + t))
+        if j == 0:
+            cx_copy(1, away, n_full).start()
         cross(j, Q,
               lambda t: jnp.where(first, OWN, NB1) + t,
               lambda t: jnp.where(first, NB1, OWN) + j,
-              lambda t: T_A + stair(t, j))
-
-    cx_copy(1, T_W, T_A).start()
-    cx_copy(2, T_A, T_C).start()
-
-    def c_even(t, _):
-        put(T_C + t, tile(PAR + t // Q, NB1 + lax.rem(t, Q)) * w_own)
-        return 0
-    lax.fori_loop(0, jnp.where(first, Q * Q, 0), c_even, 0)
-
-    cx_sum(1, T_W, T_A)
-    cx_sum(2, T_A, T_C)
-
-    @pl.when(p == 1)
-    def _():
-        remote(summed.at[T_W:T_A], got_m, m_send.at[0], m_recv.at[0], mate).start()
+              lambda t: T_A + late(t, j))
+        if j == 0:
+            cx_copy(2, T_A, n_tri).start()
+            cx_sum(1, away, n_full)
+            send_m().start()
+        cross(0, jnp.where(first, Q, 0),
+              lambda t: OWN + t,
+              lambda t: PAR + j,
+              lambda t: T_W + t * Q + j)
+
+    cx_sum(2, T_A, n_tri)
 
     @pl.when(jnp.logical_and(p == 1, dn))
     def _():
-        remote(summed.at[T_A:T_C], got_n.at[1], m_send.at[2], m_recv.at[2], to2).start()
+        send_a().start()
 
     for j in reversed(range(Q)):
+        if j == 0:
+            cx_copy(0, T_O, T_W - T_O).wait()
+            for b in range(Q):
+                for a in range(b + 1):
+                    s = T_O + stair(b, a)
+                    out[a, b - a] = (part[core, s] + cx[s]) * flag(a, b - a)
+
         @pl.when(send1)
         def _():
-            copy_b(j).wait_recv()
+            copy_b(j, 0).wait_recv()
+            copy_b(j, 1).wait_recv()
 
         @pl.when(jnp.logical_not(send1))
         def _():
             zero(NB2 + j)
 
         split(NB2 + j)
+        cross(j, Q,
+              lambda t: jnp.where(first, NB2, PAR) + t,
+              lambda t: jnp.where(first, PAR, NB2) + j,
+              lambda t: T_B + late(t, j))
+        if j == 1:
+            cx_copy(4, T_B, n_tri - Q).start()
+        if j == 0:
+            cx_copy(5, T_B + n_tri - Q, Q).start()
         cross(0, jnp.where(first, 0, Q),
               lambda t: OWN + t,
               lambda t: NB2 + j,
               lambda t: T_C + t * Q + j)
-        cross(j, Q,
-              lambda t: jnp.where(first, NB2, PAR) + t,
-              lambda t: jnp.where(first, PAR, NB2) + j,
-              lambda t: T_B + stair(t, j))
-
-    cx_copy(3, T_C, T_B).start()
-    cx_copy(4, T_B, T_END).start()
-
-    def flag(r, k):
-        return listed[r, k].astype(jnp.float32)
-
-    cx_copy(0, T_O, T_W).wait()
-    for j in range(Q):
-        for i in range(j + 1):
-            s = T_O + stair(j, i)
-            out[i, j - i] = (part[core, s] + cx[s]) * flag(i, j - i)
-
-    cx_sum(3, T_C, T_B)
-
-    @pl.when(first)
-    def _():
-        remote(summed.at[T_C:T_B], got_m, m_send.at[0], m_recv.at[0], mate).start()
-
-    cx_sum(4, T_B, T_END)
-
-    @pl.when(p == 1)
-    def _():
-        remote(summed.at[T_B:T_END], got_n.at[0], m_send.at[1], m_recv.at[1], mate).start()
-
-    @pl.when(jnp.logical_and(first, dn))
-    def _():
-        remote(summed.at[T_B:T_END], got_n.at[0], m_send.at[1], m_recv.at[1], diag).start()
-
-    remote(summed.at[T_W:T_A], got_m, m_send.at[0], m_recv.at[0], mate).wait_recv()
-    mine = jnp.where(first, T_W, T_C)
+        if j == 1:
+            cx_sum(4, T_B, n_tri - Q)
+            start_n(0)
+
+    cx_copy(3, kept, n_full).start()
+    cx_sum(5, T_B + n_tri - Q, Q)
+    start_n(1)
+    cx_sum(3, kept, n_full)
+
+    send_m().wait_recv()
     for r in range(Q):
         for c in range(Q):
-            out[r, Q + c - r] = (summed[mine + r * Q + c] + got_m[r * Q + c]) * flag(r, Q + c - r)
-
-    n_copy = remote(summed.at[T_B:T_END], got_n.at[0], m_send.at[1], m_recv.at[1], mate)
-    n_copy2 = remote(summed.at[T_A:T_C], got_n.at[1], m_send.at[2], m_recv.at[2], to2)
+            out[r, Q + c - r] = (summed[kept + r * Q + c] + got_m[r * Q + c]) * flag(r, Q + c - r)
 
     @pl.when(first)
     def _():
-        n_copy.wait_recv()
+        send_n(0, mate).wait_recv()
+        send_n(1, mate).wait_recv()
         for r in range(Q):
             for c in range(r + 1):
-                s = stair(r, c)
+                s = late(r, c)
                 out[r, 2 * Q + c - r] = (summed[T_A + s] + got_n[0, s]) * flag(r, 2 * Q + c - r)
 
     @pl.when(jnp.logical_and(p == 1, up))
     def _():
-        n_copy.wait_recv()
-        n_copy2.wait_recv()
+        send_a().wait_recv()
+        send_n(0, mate).wait_recv()
+        send_n(1, mate).wait_recv()
         for r in range(Q):
             for c in range(r + 1):
-                s = stair(r, c)
+                s = late(r, c)
                 out[r, 2 * Q + c - r] = (got_n[0, s] + got_n[1, s]) * flag(r, 2 * Q + c - r)
 
     @pl.when(jnp.logical_and(p == 1, jnp.logical_not(up)))
@@ -291,25 +322,27 @@
                 out[r, 2 * Q + c - r] = jnp.zeros((B // 2, B), jnp.float32)
 
     for j in range(Q):
-        copy_r(j).wait_send()
+        for h in range(2):
+            copy_r(j, h).wait_send()
+
+            @pl.when(send2)
+            def _():
+                copy_b(j, h).wait_send()
 
         @pl.when(send1)
         def _():
             copy_a(j).wait_send()
 
-        @pl.when(send2)
-        def _():
-            copy_b(j).wait_send()
-
-    remote(summed.at[T_W:T_A], got_m, m_send.at[0], m_recv.at[0], mate).wait_send()
+    send_m().wait_send()
 
     @pl.when(jnp.logical_or(p == 1, dn))
     def _():
-        n_copy.wait_send()
+        send_n(0, mate).wait_send()
+        send_n(1, mate).wait_send()
 
     @pl.when(jnp.logical_and(p == 1, dn))
     def _():
-        n_copy2.wait_send()
+        send_a().wait_send()
 
 
 def solution(mesh):
@@ -343,8 +376,8 @@
                 pltpu.VMEM((T_A - T_W, B // 2, B), jnp.float32),
                 pltpu.VMEM((2, T_C - T_A, B // 2, B), jnp.float32),
                 dma((2 * Q,)),
-                dma((Q,)), dma((Q,)), dma((Q,)), dma((Q,)), dma((Q,)), dma((Q,)),
-                dma((5,)), dma((5,)), dma((3,)), dma((3,)),
+                dma((2 * Q,)), dma((2 * Q,)), dma((Q,)), dma((Q,)), dma((2 * Q,)), dma((2 * Q,)),
+                dma((6,)), dma((6,)), dma((4,)), dma((4,)),
             ],
             compiler_params=pltpu.CompilerParams(
                 collective_id=0, has_side_effects=True, vmem_limit_bytes=56 * 1024 * 1024),

time: 98.2 us -> 83.5 us (0.85)
  Pallas kernels: 95.6 us -> 80.9 us
    pallas_call x1, Pallas kernels: 95.6 us -> 80.9 us  [on_device(): pl.pallas_call(functools.partial(kernel, rows_n, cols_n), out_shape=jax.S...]
where the time goes in v2:
time: 83.5 us; the launch traced here: 83.3 us
  Pallas kernels  80.9 us (97%)
  local copies, waits for them, and re-layouts  2.41 us (3%)
    pallas_call x1, Pallas kernels, on_device(): pl.pallas_call(functools.partial(kernel, rows_n, cols_n), out_shape=jax.S...  80.9 us
    unnamed x1, local copies, waits for them, and re-layouts  2.41 us

profile of v2, /device:TPU:0, one launch (start us, length us, event | category | flops | bytes accessed | tf_op | source)
XLA Modules:
  0.0 83.3 jit_solution(9797210074790122681)
XLA Ops:
  0.0 80.9 %shard_map.37 = f32[4,9,64,128]{3,2,1,0:T(8,128)} custom-call(f32[2,2,512,512]{3,2,1,0:T(8,128)} %green.1, f32[2]{0:T(128)} %weights.1, s32[4,9]{1,0:T(4,128)} %listed.1), custom_call_target="tpu_custom_call" | custom-call | tf_op jit(solution)/shard_map/pallas_call | solution.py:360
  80.9 2.4 %copy.5 = f32[4,9,64,128]{3,2,1,0:T(8,128)} copy(f32[4,9,64,128]{3,2,1,0:T(8,128)} %shard_map.37) | data formatting | bytes 2359296

commit v3 on v2

--- a/solution.py
+++ b/solution.py
@@ -15,6 +15,7 @@
 
 OWN, OTH, PAR, NB1, NB2 = 0, 4, 8, 12, 16
 T_O, T_W, T_A, T_C, T_B, T_END = 0, 10, 26, 36, 52, 62
+GROUP = 2
 
 
 def stair(r, c):
@@ -117,18 +118,20 @@
                 hi[slot, B:2 * B, b:b + ns] = -xh if part_i == 1 else xh
                 lo[slot, B:2 * B, b:b + ns] = -xl if part_i == 1 else xl
 
-    def gram(rs, cs, h):
+    def gram(rs, n, cs, h):
         k = slice(h * 2 * ns, (h + 1) * 2 * ns)
-        xh, xl, yh, yl = hi[rs, 0:B, k], lo[rs, 0:B, k], hi[cs, :, k], lo[cs, :, k]
+        xh = hi[pl.ds(rs, n), 0:B, k].reshape(n * B, 2 * ns)
+        xl = lo[pl.ds(rs, n), 0:B, k].reshape(n * B, 2 * ns)
 
         def dot(x, y):
             return lax.dot_general(x, y, (((1,), (1,)), ((), ())), preferred_element_type=jnp.float32)
 
-        return dot(xh, yh) + (dot(xh, yl) + dot(xl, yh))
-
-    def tile(rs, cs):
-        s = gram(rs, cs, 0)
-        r = gram(rs, cs, 1)
+        both = dot(jnp.concatenate([xh, xl], 0), hi[cs, :, k])
+        return both[:n * B] + (both[n * B:] + dot(xh, lo[cs, :, k]))
+
+    def tiles(rs, n, cs):
+        s = gram(rs, n, cs, 0)
+        r = gram(rs, n, cs, 1)
         return s[:, :B] * r[:, :B] - s[:, B:] * r[:, B:]
 
     scale = 1.0 / math.sqrt(ns * (nsr - ns))
@@ -139,11 +142,15 @@
         part[0, slot] = value[:B // 2]
         part[1, slot] = value[B // 2:]
 
-    def cross(start, stop, row_of, col_of, slot_of):
-        def body(t, _):
-            put(slot_of(t), tile(row_of(t), col_of(t)) * w_own)
-            return 0
-        lax.fori_loop(start, stop, body, 0)
+    def runs(start, stop):
+        return [(t, min(GROUP, stop - t)) for t in range(start, stop, GROUP)]
+
+    def cross(start, stop, row, col, slot_of, flip=False):
+        for t, n in runs(start, stop):
+            value = tiles(row + t, n, col) * w_own
+            for i in range(n):
+                one = value[i * B:(i + 1) * B]
+                put(slot_of(t + i), one.T if flip else one)
 
     def cx_copy(i, a, n):
         return remote(part.at[1 - core, pl.ds(a, n)], cx.at[pl.ds(a, n)], c_send.at[i], c_recv.at[i], twin)
@@ -166,10 +173,10 @@
     lax.fori_loop(0, 2 * Q, split_own, 0)
 
     for j in range(Q):
-        def body(i, _, j=j):
-            put(T_O + stair(j, i), tile(OWN + i, OWN + j) * w_own + tile(OTH + i, OTH + j) * w_oth)
-            return 0
-        lax.fori_loop(0, j + 1, body, 0)
+        for t, n in runs(0, j + 1):
+            value = tiles(OWN + t, n, OWN + j) * w_own + tiles(OTH + t, n, OTH + j) * w_oth
+            for i in range(n):
+                put(T_O + stair(j, t + i), value[i * B:(i + 1) * B])
     cx_copy(0, T_O, T_W - T_O).start()
 
     def zero(slot):
@@ -221,30 +228,26 @@
 
         split(NB1 + j)
 
-        def cr(t):
-            return jnp.where(t < Q - j, j, t - (Q - j) + j + 1)
-
-        def cc(t):
-            return jnp.where(t < Q - j, j + t, j)
-
-        cross(0, jnp.where(first, 2 * (Q - j) - 1, Q),
-              lambda t: jnp.where(first, PAR + cr(t), PAR + j),
-              lambda t: jnp.where(first, NB1 + cc(t), OWN + t),
-              lambda t: jnp.where(first, T_C + cr(t) * Q + cc(t), T_W + j * Q + t))
+        @pl.when(first)
+        def _():
+            cross(j, Q, PAR, NB1 + j, lambda t: T_C + t * Q + j)
+            cross(j + 1, Q, NB1, PAR + j, lambda t: T_C + j * Q + t, flip=True)
+
+        @pl.when(p == 1)
+        def _():
+            cross(0, Q, OWN, PAR + j, lambda t: T_W + j * Q + t, flip=True)
+
         if j == 0:
             cx_copy(1, away, n_full).start()
-        cross(j, Q,
-              lambda t: jnp.where(first, OWN, NB1) + t,
-              lambda t: jnp.where(first, NB1, OWN) + j,
-              lambda t: T_A + late(t, j))
+        cross(j, Q, jnp.where(first, OWN, NB1), jnp.where(first, NB1, OWN) + j, lambda t: T_A + late(t, j))
         if j == 0:
             cx_copy(2, T_A, n_tri).start()
             cx_sum(1, away, n_full)
             send_m().start()
-        cross(0, jnp.where(first, Q, 0),
-              lambda t: OWN + t,
-              lambda t: PAR + j,
-              lambda t: T_W + t * Q + j)
+
+        @pl.when(first)
+        def _():
+            cross(0, Q, OWN, PAR + j, lambda t: T_W + t * Q + j)
 
     cx_sum(2, T_A, n_tri)
 
@@ -270,18 +273,16 @@
             zero(NB2 + j)
 
         split(NB2 + j)
-        cross(j, Q,
-              lambda t: jnp.where(first, NB2, PAR) + t,
-              lambda t: jnp.where(first, PAR, NB2) + j,
-              lambda t: T_B + late(t, j))
+        cross(j, Q, jnp.where(first, NB2, PAR), jnp.where(first, PAR, NB2) + j, lambda t: T_B + late(t, j))
         if j == 1:
             cx_copy(4, T_B, n_tri - Q).start()
         if j == 0:
             cx_copy(5, T_B + n_tri - Q, Q).start()
-        cross(0, jnp.where(first, 0, Q),
-              lambda t: OWN + t,
-              lambda t: NB2 + j,
-              lambda t: T_C + t * Q + j)
+
+        @pl.when(p == 1)
+        def _():
+            cross(0, Q, OWN, NB2 + j, lambda t: T_C + t * Q + j)
+
         if j == 1:
             cx_sum(4, T_B, n_tri - Q)
             start_n(0)

time: 83.5 us -> 78.3 us (0.938)
  Pallas kernels: 80.9 us -> 75.7 us
    pallas_call x1, Pallas kernels: 80.9 us -> 75.7 us  [on_device(): pl.pallas_call(functools.partial(kernel, rows_n, cols_n), out_shape=jax.S...]
where the time goes in v3:
time: 78.3 us; the launch traced here: 78.1 us
  Pallas kernels  75.7 us (97%)
  local copies, waits for them, and re-layouts  2.41 us (3%)
    pallas_call x1, Pallas kernels, on_device(): pl.pallas_call(functools.partial(kernel, rows_n, cols_n), out_shape=jax.S...  75.7 us
    unnamed x1, local copies, waits for them, and re-layouts  2.41 us

profile of v3, /device:TPU:0, one launch (start us, length us, event | category | flops | bytes accessed | tf_op | source)
XLA Modules:
  0.0 78.1 jit_solution(380859264047247128)
XLA Ops:
  0.0 75.7 %shard_map.37 = f32[4,9,64,128]{3,2,1,0:T(8,128)} custom-call(f32[2,2,512,512]{3,2,1,0:T(8,128)} %green.1, f32[2]{0:T(128)} %weights.1, s32[4,9]{1,0:T(4,128)} %listed.1), custom_call_target="tpu_custom_call" | custom-call | tf_op jit(solution)/shard_map/pallas_call | solution.py:361
  75.7 2.4 %copy.5 = f32[4,9,64,128]{3,2,1,0:T(8,128)} copy(f32[4,9,64,128]{3,2,1,0:T(8,128)} %shard_map.37) | data formatting | bytes 2359296
